TPU v7x, 1024 devices: a whole 4x4x32 slice. The times are simulated.
1024 devices in a mesh: ep: 32 (over x, y, core), dp: 32 (over z).
Axes of the slice: x: 4, y: 4, z: 32, core: 2. Of those that a mesh axis runs over, the one named last changes fastest.
Arguments:
- rows_in: bfloat16 [131072, 2048], P(('ep', 'dp')), may hold values from -3 to 3
- grads_in: bfloat16 [131072, 2048], P(('ep', 'dp')), may hold values from -3 to 3
- expert_ids: int32 [131072, 1], P(('ep', 'dp')), may hold values from 0 to 31; in each aligned block of 128 rows (0 to 127, 128 to 255, ...) at most 8 rows name the same one
- w_gate: bfloat16 [32, 2048, 640], P('ep'), may hold values from -0.125 to 0.125
- w_up: bfloat16 [32, 2048, 640], P('ep'), may hold values from -0.125 to 0.125
- w_down: bfloat16 [32, 640, 2048], P('ep'), may hold values from -0.25 to 0.25
- project: bfloat16 [32, 2, 2048, 64], P('ep'), may hold values from -0.75 to 0.75
- moment_one: float32 [32, 122880], P('ep', 'dp'), may hold values from -3 to 3
- moment_two: float32 [32, 122880], P('ep', 'dp'), may hold values from 0.01 to 0.3
Outputs:
- rows_out: bfloat16 [131072, 2048], P(('ep', 'dp'))
- first_new: float32 [32, 122880], P('ep', 'dp')
- second_new: float32 [32, 122880], P('ep', 'dp')
- step_gate: bfloat16 [32, 2048, 640], P('ep', 'dp')
- step_up: bfloat16 [32, 2048, 640], P('ep', 'dp')
- step_down: bfloat16 [32, 640, 2048], P('ep', None, 'dp')
Inputs may be any that keep to these rules, and one draw needn't show every extreme that they name: `expert_ids`: within the 128 rows of one device no expert is named by more than 8 rows, and some devices name one expert by exactly 8 rows.
All inputs are finite; a program needn't handle non-finite values.
Results may differ from a plain program's by a relative error of at most 0.0049.
Values may be sent and summed in bfloat16 or wider, within the bound.
A program may use at most 64 MiB of HBM per device.

v0:
```python
import math

import jax
import jax.numpy as jnp
from jax import lax
from jax.sharding import PartitionSpec as P

beta_one = 0.9
beta_two = 0.999
adam_eps = 1e-08
bias_one = 1.0 - 0.9**10
bias_two = 1.0 - 0.999**10
highest = lax.Precision.HIGHEST


def slot_places(targets, capacity):
    row_count = targets.shape[0]
    positions = lax.iota(jnp.int32, row_count)
    same_before = (targets[:, None] == targets[None, :]) & (positions[:, None] > positions[None, :])
    ranked = jnp.sum(same_before.astype(jnp.int32), axis=1)
    return targets * capacity + ranked


def forward_again(rows_x, gate_mat, up_mat):
    gate_pre = jnp.dot(rows_x, gate_mat, preferred_element_type=jnp.float32)
    up_pre = jnp.dot(rows_x, up_mat, preferred_element_type=jnp.float32)
    sigmoid = jax.nn.sigmoid(gate_pre)
    hidden = (gate_pre * sigmoid * up_pre).astype(jnp.bfloat16)
    return (gate_pre, up_pre, sigmoid, hidden)


def backward_pass(
    rows_x, rows_g, gate_pre, up_pre, sigmoid, hidden, gate_mat, up_mat, down_mat, proj_mats
):
    hidden_grad = jnp.einsum("sd,fd->sf", rows_g, down_mat, preferred_element_type=jnp.float32)
    up_grad = (hidden_grad * gate_pre * sigmoid).astype(jnp.bfloat16)
    gate_grad = (hidden_grad * up_pre * sigmoid * (1.0 + gate_pre * (1.0 - sigmoid))).astype(
        jnp.bfloat16
    )
    rows_grad = (
        jnp.einsum("sf,df->sd", gate_grad, gate_mat, preferred_element_type=jnp.float32)
        + jnp.einsum("sf,df->sd", up_grad, up_mat, preferred_element_type=jnp.float32)
    ).astype(jnp.bfloat16)
    proj_in = jnp.dot(rows_x, proj_mats[0], preferred_element_type=jnp.float32)
    proj_down = jnp.dot(rows_g, proj_mats[1], preferred_element_type=jnp.float32)
    grad_gate = jnp.einsum("sr,sf->rf", proj_in, gate_grad.astype(jnp.float32), precision=highest)
    grad_up = jnp.einsum("sr,sf->rf", proj_in, up_grad.astype(jnp.float32), precision=highest)
    grad_down = jnp.einsum("sr,sf->rf", proj_down, hidden.astype(jnp.float32), precision=highest)
    return (rows_grad, jnp.stack([grad_gate, grad_up, grad_down]))


def adam_rule(grad_part, first_old, second_old):
    first_new = beta_one * first_old + (1.0 - beta_one) * grad_part
    second_new = beta_two * second_old + (1.0 - beta_two) * grad_part * grad_part
    update = first_new / bias_one / (jnp.sqrt(second_new / bias_two) + adam_eps)
    return (first_new, second_new, update)


def local(rows_in, grads_in, expert_ids, w_gate, w_up, w_down, project, moment_one, moment_two):
    ep_count = lax.axis_size("ep")
    dp_count = lax.axis_size("dp")
    rows_dev = rows_in.shape[0]
    width = rows_in.shape[1]
    capacity = 2 * rows_dev // ep_count
    places = slot_places(expert_ids[:, 0], capacity)
    empty_slots = jnp.zeros((ep_count * capacity, width), jnp.bfloat16)
    send_rows = empty_slots.at[places].set(rows_in)
    send_grads = empty_slots.at[places].set(grads_in)
    gate_mat = w_gate[0]
    up_mat = w_up[0]
    down_mat = w_down[0]
    proj_mats = project[0]
    recv_rows, recv_grads = (
        lax.all_to_all(send_rows, "ep", split_axis=0, concat_axis=0, tiled=True),
        lax.all_to_all(send_grads, "ep", split_axis=0, concat_axis=0, tiled=True),
    )
    gate_pre, up_pre, sigmoid, hidden = forward_again(recv_rows, gate_mat, up_mat)
    rows_grad, grad_terms = backward_pass(
        recv_rows,
        recv_grads,
        gate_pre,
        up_pre,
        sigmoid,
        hidden,
        gate_mat,
        up_mat,
        down_mat,
        proj_mats,
    )
    returned = lax.all_to_all(rows_grad, "ep", split_axis=0, concat_axis=0, tiled=True)
    rows_out = returned[places]
    total_rows = rows_dev * ep_count * dp_count
    grad_flat = grad_terms.reshape(-1) * (1.0 / math.sqrt(total_rows))
    share = moment_one.shape[1]
    dp_index = lax.axis_index("dp")
    grad_sum = lax.psum(grad_flat, "dp")
    first_all, second_all = (
        lax.all_gather(moment_one, "dp", axis=1, tiled=True),
        lax.all_gather(moment_two, "dp", axis=1, tiled=True),
    )
    first_whole, second_whole, update = adam_rule(grad_sum, first_all[0], second_all[0])
    first_new = lax.dynamic_slice_in_dim(first_whole, dp_index * share, share)[None]
    second_new = lax.dynamic_slice_in_dim(second_whole, dp_index * share, share)[None]
    update = update.reshape(grad_terms.shape)
    slab = width // dp_count
    proj_rows = lax.dynamic_slice_in_dim(proj_mats, dp_index * slab, slab, axis=1).astype(
        jnp.float32
    )
    step_gate = jnp.dot(proj_rows[0], update[0], precision=highest).astype(jnp.bfloat16)[None]
    step_up = jnp.dot(proj_rows[0], update[1], precision=highest).astype(jnp.bfloat16)[None]
    step_down = jnp.einsum("rf,dr->fd", update[2], proj_rows[1], precision=highest).astype(
        jnp.bfloat16
    )[None]
    return (rows_out, first_new, second_new, step_gate, step_up, step_down)


def solution(mesh):
    in_specs = (
        P(("ep", "dp"), None),
        P(("ep", "dp"), None),
        P(("ep", "dp"), None),
        P("ep", None, None),
        P("ep", None, None),
        P("ep", None, None),
        P("ep", None, None, None),
        P("ep", "dp"),
        P("ep", "dp"),
    )
    out_specs = (
        P(("ep", "dp"), None),
        P("ep", "dp"),
        P("ep", "dp"),
        P("ep", "dp", None),
        P("ep", "dp", None),
        P("ep", None, "dp"),
    )
    return jax.shard_map(local, mesh=mesh, in_specs=in_specs, out_specs=out_specs, check_vma=False)
```

profile of v0, /device:TPU:6, one launch (start us, length us, event | category | flops | bytes accessed | tf_op | source)
XLA Modules:
  0.0 455.9 jit_solution(3504702061508388493)
XLA Ops:
  7.2 0.0 copy-start
  7.2 0.0 copy-start.5
  7.2 0.0 copy-start.6
  7.2 1.0 convert_reduce_fusion
  8.2 0.7 fusion.35
  8.9 2.9 scatter_custom_fusion.1
  11.8 17.5 %all-to-all-start.1 = ((bf16[32,8,2048]{2,1,0:T(8,128)(2,1)}), bf16[32,8,2048]{2,1,0:T(8,128)(2,1)}, u32[]{:S(2)}, u32[]{:S(2)}) async-start(bf16[32,8,2048]{2,1,0:T(8,128)(2,1)} %bitcast.83), calls=%async_computation.1 | async-start | bytes 2097152 | tf_op jit(solution)/shard_map/all_to_all | solution.py:74
  29.3 0.0 copy-done.5
  29.4 60.7 %all_gather.6 = f32[1,122880]{1,0:T(1,128)S(1)} all-gather(f32[1,3840]{1,0:T(1,128)S(1)} %copy-done.5), channel_id=1, replica_groups=mesh['ep'=32,'dp'=32] {'dp'}, dimensions={1}, use_global_device_ids=true | all-gather | bytes 506880 | tf_op jit(solution)/shard_map/all_gather | solution.py:98
  90.0 0.5 broadcast_multiply_fusion.1
  90.5 0.0 copy-done.6
  90.6 53.8 %all_gather.7 = f32[1,122880]{1,0:T(1,128)S(1)} all-gather(f32[1,3840]{1,0:T(1,128)S(1)} %copy-done.6), channel_id=1, replica_groups=mesh['ep'=32,'dp'=32] {'dp'}, dimensions={1}, use_global_device_ids=true | all-gather | bytes 506880 | tf_op jit(solution)/shard_map/all_gather | solution.py:99
  144.4 1.3 broadcast_multiply_fusion
  145.7 3.0 scatter_custom_fusion
  148.7 0.0 all-to-all-done.1
  148.7 7.6 %all-to-all-start = ((bf16[32,8,2048]{2,1,0:T(8,128)(2,1)}), bf16[32,8,2048]{2,1,0:T(8,128)(2,1)}, u32[]{:S(2)}, u32[]{:S(2)}) async-start(bf16[32,8,2048]{2,1,0:T(8,128)(2,1)} %bitcast.82), calls=%async_computation | async-start | bytes 2097152 | tf_op jit(solution)/shard_map/all_to_all | solution.py:75
  156.3 0.0 all-reduce.2.cloned.1.call-start
  156.4 1.7 fusion.18
  158.1 0.0 copy-start.1
  158.1 3.2 fusion.2
  161.3 3.0 fusion.5
  164.3 7.3 %all-to-all-done = bf16[32,8,2048]{2,1,0:T(8,128)(2,1)} async-done(((bf16[32,8,2048]{2,1,0:T(8,128)(2,1)}), bf16[32,8,2048]{2,1,0:T(8,128)(2,1)}, u32[]{:S(2)}, u32[]{:S(2)}) %all-to-all-start) | async-done | bytes 1048608 | tf_op jit(solution)/shard_map/all_to_all | solution.py:75
  171.6 3.6 multiply_convert_fusion.1
  175.3 0.0 copy-start.3
  175.3 0.3 convolution_bitcast_fusion.1
  175.6 0.3 convolution_bitcast_fusion.2
  175.8 1.7 fusion.22
  177.5 0.0 copy-done.7
  177.5 0.4 convolution_bitcast_fusion
  178.0 0.0 copy-done.3
  178.0 0.8 maximum_multiply_fusion
  178.8 1.9 mul.95
  180.7 0.0 all-reduce.2.cloned.1.call-update
  180.7 0.0 copy-start.2
  180.7 2.1 fusion
  182.8 2.0 fusion.12
  184.9 6.1 %all-to-all-start.2 = ((bf16[32,8,2048]{2,1,0:T(8,128)(2,1)}), bf16[32,8,2048]{2,1,0:T(8,128)(2,1)}, u32[]{:S(2)}, u32[]{:S(2)}) async-start(bf16[32,8,2048]{2,1,0:T(8,128)(2,1)} %fusion.12), calls=%async_computation.2 | async-start | bytes 2097152 | tf_op jit(solution)/shard_map/all_to_all | solution.py:90
  191.0 244.0 %all-reduce.2.cloned.1.call-done = f32[122880]{0:T(1024)} async-done(((f32[122880]{0:T(1024)}), f32[122880]{0:T(1024)}) %all-reduce.2.cloned.1.call-update) | async-done | bytes 491536 | tf_op jit(solution)/shard_map/psum | solution.py:96
  435.0 2.4 add_divide_fusion.1
  437.5 0.8 dynamic_slice.10
  438.3 0.6 broadcast_in_dim.25
  439.0 0.8 dynamic_slice.9
  439.8 0.6 broadcast_in_dim.24
  440.4 1.7 fusion.15
  442.1 1.7 fusion.16
  443.8 1.7 fusion.17
  445.5 0.0 all-to-all-done.2
  445.5 3.6 gather_fusion
  (13 shorter events, 0.2 us)
Async XLA Ops:
  7.2 150.9 %copy-start = (bf16[1,2048,640]{2,1,0:T(8,128)(2,1)S(1)}, bf16[1,2048,640]{2,1,0:T(8,128)(2,1)}, u32[]{:S(2)}) copy-start(bf16[1,2048,640]{2,1,0:T(8,128)(2,1)} %param.12) | copy-start | bytes 7864324
  7.2 22.2 %copy-start.5 = (f32[1,3840]{1,0:T(1,128)S(1)}, f32[1,3840]{1,0:T(1,128)}, u32[]{:S(2)}) copy-start(f32[1,3840]{1,0:T(1,128)} %param.16) | copy-start | bytes 46084
  7.2 83.4 %copy-start.6 = (f32[1,3840]{1,0:T(1,128)S(1)}, f32[1,3840]{1,0:T(1,128)}, u32[]{:S(2)}) copy-start(f32[1,3840]{1,0:T(1,128)} %param.17) | copy-start | bytes 46084
  11.8 136.8 %all-to-all-start.1 = ((bf16[32,8,2048]{2,1,0:T(8,128)(2,1)}), bf16[32,8,2048]{2,1,0:T(8,128)(2,1)}, u32[]{:S(2)}, u32[]{:S(2)}) async-start(bf16[32,8,2048]{2,1,0:T(8,128)(2,1)} %bitcast.83), calls=%async_computation.1 | async-start | bytes 2097152 | tf_op jit(solution)/shard_map/all_to_all | solution.py:74
  148.7 23.0 %all-to-all-start = ((bf16[32,8,2048]{2,1,0:T(8,128)(2,1)}), bf16[32,8,2048]{2,1,0:T(8,128)(2,1)}, u32[]{:S(2)}, u32[]{:S(2)}) async-start(bf16[32,8,2048]{2,1,0:T(8,128)(2,1)} %bitcast.82), calls=%async_computation | async-start | bytes 2097152 | tf_op jit(solution)/shard_map/all_to_all | solution.py:75
  156.3 278.7 %all-reduce.2.cloned.1.call-start = ((), (), s32[]{:S(2)}) async-start(), calls=%async_computation.3 | async-start | bytes 983040 | tf_op jit(solution)/shard_map/psum | solution.py:96
  158.1 3.2 copy-start.1
  171.6 4.2 copy-start.4
  171.6 5.9 %copy-start.7 = (f32[256,640]{1,0:T(8,128)S(1)}, f32[256,640]{1,0:T(8,128)}, u32[]{:S(2)}) copy-start(f32[256,640]{1,0:T(8,128)} %fusion.2) | copy-start | bytes 1966084
  171.6 5.9 %copy-start.8 = (f32[256,640]{1,0:T(8,128)S(1)}, f32[256,640]{1,0:T(8,128)}, u32[]{:S(2)}) copy-start(f32[256,640]{1,0:T(8,128)} %fusion.5) | copy-start | bytes 1966084
  175.3 2.7 copy-start.3
  180.7 2.1 copy-start.2
  184.9 260.6 %all-to-all-start.2 = ((bf16[32,8,2048]{2,1,0:T(8,128)(2,1)}), bf16[32,8,2048]{2,1,0:T(8,128)(2,1)}, u32[]{:S(2)}, u32[]{:S(2)}) async-start(bf16[32,8,2048]{2,1,0:T(8,128)(2,1)} %fusion.12), calls=%async_computation.2 | async-start | bytes 2097152 | tf_op jit(solution)/shard_map/all_to_all | solution.py:90
Sparse Core Ops, SparseCore 0:
  180.8 254.1 all-reduce.1
where the time goes:
time: 457 us; the launch traced here: 456 us
  waiting for transfers between devices  251 us (55%)
  blocking collectives  115 us (25%)
  starting transfers between devices  31.3 us (7%)
  matrix products  23.5 us (5%)
  local copies, waits for them, and re-layouts  14.4 us (3%)
  between operations  14.2 us (3%)
  other arithmetic  6.67 us (1%)
    psum x1, waiting for transfers between devices, local(): grad_sum = lax.psum(grad_flat, 'dp')  244 us
    all_gather x1, blocking collectives, local(): lax.all_gather(moment_one, 'dp', axis=1, tiled=True)  60.7 us
    all_gather x1, blocking collectives, local(): lax.all_gather(moment_two, 'dp', axis=1, tiled=True)  53.8 us
    all_to_all x1, starting transfers between devices, local(): lax.all_to_all(send_rows, 'ep', split_axis=0, concat_axis=0, tiled=True)  17.5 us
  transfers between devices with their start and end apart: 4, of which 2 were waited for; matrix products, arithmetic and copies ran while one was open for 6% of the time, Pallas kernels for 0%

commit v1 on v0

v1 whole, which is shorter than its diff:
```python
import functools
import math

import jax
import jax.numpy as jnp
from jax import lax
from jax.experimental import pallas as pl
from jax.experimental.pallas import tpu as pltpu
from jax.sharding import PartitionSpec as P

beta_one = 0.9
beta_two = 0.999
adam_eps = 1e-08
bias_one = 1.0 - 0.9**10
bias_two = 1.0 - 0.999**10

MESH = pl.DeviceIdType.MESH
CAP = 8
GROUP = 4
LANES = 128
F32 = jnp.float32
BF16 = jnp.bfloat16


def dot(a, b):
    return jnp.dot(a, b, preferred_element_type=F32)


def dot_nt(a, b):
    return lax.dot_general(a, b, (((1,), (1,)), ((), ())), preferred_element_type=F32)


def dot_tn(a, b):
    return lax.dot_general(a, b, (((0,), (0,)), ((), ())), preferred_element_type=F32)


def remote(src, dst, send_sem, recv_sem, **device):
    return pltpu.make_async_remote_copy(
        src_ref=src,
        dst_ref=dst,
        send_sem=send_sem,
        recv_sem=recv_sem,
        device_id=device,
        device_id_type=MESH,
    )


def blocks_of(total, width):
    return [(at, min(width, total - at)) for at in range(0, total, width)]


def kernel(
    n_ep,
    n_dp,
    scale,
    ids_ref,
    m1_ref,
    m2_ref,
    x_hbm,
    g_hbm,
    wg_hbm,
    wu_hbm,
    wd_hbm,
    proj_hbm,
    rows_ref,
    first_ref,
    second_ref,
    step_gate_ref,
    step_up_ref,
    step_down_ref,
    x_in,
    g_in,
    wg,
    wu,
    wd,
    proj,
    x_send,
    g_send,
    x_got,
    g_got,
    back_send,
    back_got,
    act_a,
    act_b,
    hidden,
    grads,
    grad_pad,
    chunk_wide,
    part_send,
    part_got,
    sum_send,
    sum_got,
    upd_all,
    upd_pad,
    mom,
    local_sem,
    x_ss,
    x_rs,
    g_ss,
    g_rs,
    b_ss,
    b_rs,
    p_ss,
    p_rs,
    s_ss,
    s_rs,
    u_ss,
    u_rs,
    v_ss,
    v_rs,
):
    ep = lax.axis_index("ep")
    dp = lax.axis_index("dp")
    rows_dev, width = x_in.shape
    ff = wg.shape[1]
    rank = proj.shape[1]
    slots = n_ep * CAP
    n_class = n_dp // GROUP
    per_chunk = 3 * rank // n_dp
    wide = ff // LANES
    chunk_rows = chunk_wide.shape[0] // n_dp
    slab = width // n_dp
    mine_a = dp // GROUP
    mine_b = lax.rem(dp, GROUP)

    loads = [
        pltpu.make_async_copy(x_hbm, x_in, local_sem.at[0]),
        pltpu.make_async_copy(g_hbm, g_in, local_sem.at[1]),
        pltpu.make_async_copy(proj_hbm, proj, local_sem.at[2]),
        pltpu.make_async_copy(wg_hbm, wg, local_sem.at[3]),
        pltpu.make_async_copy(wu_hbm, wu, local_sem.at[4]),
        pltpu.make_async_copy(wd_hbm, wd, local_sem.at[5]),
    ]
    for load in loads:
        load.start()

    barrier = pltpu.get_barrier_semaphore()

    def greet(k, carry):
        pl.semaphore_signal(
            barrier, inc=1, device_id={"ep": lax.rem(ep + k, n_ep)}, device_id_type=MESH
        )
        return carry

    lax.fori_loop(1, n_ep, greet, 0)
    for k in range(1, GROUP):
        peer = mine_a * GROUP + lax.rem(mine_b + k, GROUP)
        pl.semaphore_signal(barrier, inc=1, device_id={"dp": peer}, device_id_type=MESH)
    for k in range(1, n_class):
        peer = lax.rem(mine_a + k, n_class) * GROUP + mine_b
        pl.semaphore_signal(barrier, inc=1, device_id={"dp": peer}, device_id_type=MESH)

    ids = ids_ref[...]
    named = (lax.broadcasted_iota(jnp.int32, (n_ep, rows_dev), 0) == ids).astype(F32)
    before = lax.broadcasted_iota(jnp.int32, (rows_dev, rows_dev), 0) < lax.broadcasted_iota(
        jnp.int32, (rows_dev, rows_dev), 1
    )
    counts = dot(named.astype(BF16), before.astype(F32).astype(BF16))
    ranked = jnp.sum(named * counts, axis=0, keepdims=True)
    place = ids * CAP + ranked.astype(jnp.int32)
    spread32 = (lax.broadcasted_iota(jnp.int32, (slots, rows_dev), 0) == place).astype(F32)
    spread = spread32.astype(BF16)
    gather = spread32.T.astype(BF16)

    def scatter(source, target):
        for at, size in blocks_of(width, 512):
            block = dot(spread, source[:, at : at + size])
            target[:, :, at : at + size] = block.reshape(n_ep, CAP, size).astype(BF16)

    def send_all(source, target, send_sems, recv_sems):
        pltpu.make_async_copy(source.at[ep], target.at[0], recv_sems.at[0]).start()

        def one(k, carry):
            to = lax.rem(ep + k, n_ep)
            remote(
                source.at[to], target.at[k], send_sems.at[k], recv_sems.at[k], ep=to
            ).start()
            return carry

        lax.fori_loop(1, n_ep, one, 0)

    def wait_all(source, target, send_sems, recv_sems):
        pltpu.make_async_copy(source.at[ep], target.at[0], recv_sems.at[0]).wait()

        def one(k, carry):
            to = lax.rem(ep + k, n_ep)
            remote(
                source.at[to], target.at[k], send_sems.at[k], recv_sems.at[k], ep=to
            ).wait_recv()
            return carry

        lax.fori_loop(1, n_ep, one, 0)

    loads[0].wait()
    scatter(x_in, x_send)
    pl.semaphore_wait(barrier, (n_ep - 1) + (GROUP - 1) + (n_class - 1))
    send_all(x_send, x_got, x_ss, x_rs)
    loads[1].wait()
    scatter(g_in, g_send)
    send_all(g_send, g_got, g_ss, g_rs)

    def owner_of(position):
        return lax.rem(position, n_class) * GROUP + position // n_class

    pad_row = lax.broadcasted_iota(jnp.int32, (8 * n_dp, 3 * rank), 0)
    pad_col = lax.broadcasted_iota(jnp.int32, (8 * n_dp, 3 * rank), 1)
    within = lax.rem(pad_row, 8)
    pick = (pad_col == owner_of(pad_row // 8) * per_chunk + within) & (within < per_chunk)
    pick = pick.astype(F32).astype(BF16)
    sel_row = lax.broadcasted_iota(jnp.int32, (3 * rank, 8 * n_dp), 0)
    sel_col = lax.broadcasted_iota(jnp.int32, (3 * rank, 8 * n_dp), 1)
    within = lax.rem(sel_col, 8)
    place_back = (sel_row == owner_of(sel_col // 8) * per_chunk + within) & (within < per_chunk)
    place_back = place_back.astype(F32).astype(BF16)
    loads[2].wait()
    lane_at = pl.multiple_of((dp * slab) // LANES * LANES, LANES)
    part_at = lax.rem(dp * slab, LANES) // slab
    steps_lhs = []
    for kind in range(3):
        piece = proj[min(kind, 2) // 2, :, pl.ds(lane_at, LANES)]
        both = dot_tn(piece, place_back[kind * rank : (kind + 1) * rank])
        chosen = both[0:slab]
        for other in range(1, LANES // slab):
            chosen = jnp.where(part_at == other, both[other * slab : (other + 1) * slab], chosen)
        steps_lhs.append(chosen.astype(BF16))
    steps_lhs = jnp.concatenate(steps_lhs, axis=0)
    mom[...] = jnp.zeros_like(mom)
    for o in range(per_chunk):
        for l in range(wide):
            lanes = slice(o * ff + l * LANES, o * ff + (l + 1) * LANES)
            row = l * per_chunk + o
            mom[0, row : row + 1, :] = m1_ref[:, lanes]
            mom[1, row : row + 1, :] = m2_ref[:, lanes]

    loads[3].wait()
    loads[4].wait()
    loads[5].wait()
    wait_all(x_send, x_got, x_ss, x_rs)
    got = x_got[...].reshape(slots, width)
    for at, size in blocks_of(ff, 256):
        gate_pre = dot(got, wg[:, at : at + size])
        up_pre = dot(got, wu[:, at : at + size])
        sigmoid = 1.0 / (1.0 + jnp.exp(-gate_pre))
        gated = gate_pre * sigmoid
        hidden[:, at : at + size] = (gated * up_pre).astype(BF16)
        act_a[:, at : at + size] = up_pre * sigmoid * (1.0 + gate_pre * (1.0 - sigmoid))
        act_b[:, at : at + size] = gated
    proj_in = dot_nt(proj[0], got)

    def halves(value):
        high = value.astype(BF16)
        return jnp.concatenate([high, (value - high.astype(F32)).astype(BF16)], axis=0)

    proj_in = halves(proj_in)

    wait_all(g_send, g_got, g_ss, g_rs)
    got = g_got[...].reshape(slots, width)
    for at, size in blocks_of(ff, 256):
        hidden_grad = dot_nt(got, wd[at : at + size, :])
        grads[:, at : at + size] = (hidden_grad * act_a[:, at : at + size]).astype(BF16)
        grads[:, ff + at : ff + at + size] = (hidden_grad * act_b[:, at : at + size]).astype(BF16)
    proj_down = halves(dot_nt(proj[1], got))
    terms = []
    for left, right in (
        (proj_in, grads[:, 0:ff]),
        (proj_in, grads[:, ff : 2 * ff]),
        (proj_down, hidden[...]),
    ):
        both = dot(left, right)
        terms.append(((both[0:rank] + both[rank : 2 * rank]) * scale).astype(BF16))
    grad_pad[...] = dot(pick, jnp.concatenate(terms, axis=0))
    for j in range(n_dp):
        for l in range(wide):
            at = j * chunk_rows + l * per_chunk
            chunk_wide[at : at + 8, :] = grad_pad[
                8 * j : 8 * j + 8, l * LANES : (l + 1) * LANES
            ]
    part_send[...] = chunk_wide[...].reshape(n_dp, chunk_rows, LANES).astype(BF16)

    part_copies = []
    for k in range(1, GROUP):
        to = lax.rem(mine_b + k, GROUP)
        part_copies.append(
            remote(
                part_send.at[pl.ds(to * n_class, n_class)],
                part_got.at[k - 1],
                p_ss.at[k],
                p_rs.at[k],
                dp=mine_a * GROUP + to,
            )
        )
    for copy in part_copies:
        copy.start()

    for at, size in blocks_of(width, 256):
        total = dot_nt(grads[:, 0:ff], wg[at : at + size, :]) + dot_nt(
            grads[:, ff : 2 * ff], wu[at : at + size, :]
        )
        back_send[:, :, at : at + size] = total.reshape(n_ep, CAP, size).astype(BF16)
    pltpu.make_async_copy(back_send.at[0], back_got.at[ep], b_rs.at[0]).start()

    def back_copy(k):
        to = lax.rem(ep + n_ep - k, n_ep)
        return remote(back_send.at[k], back_got.at[ep], b_ss.at[k], b_rs.at[k], ep=to)

    def back_start(k, carry):
        back_copy(k).start()
        return carry

    lax.fori_loop(1, n_ep, back_start, 0)

    for copy in part_copies:
        copy.wait_recv()
    total = part_send[pl.ds(mine_b * n_class, n_class)].astype(F32)
    for k in range(1, GROUP):
        total = total + part_got[k - 1].astype(F32)
    sum_send[...] = total.astype(BF16)
    sum_copies = []
    for k in range(1, n_class):
        to = lax.rem(mine_a + k, n_class)
        sum_copies.append(
            remote(
                sum_send.at[to], sum_got.at[k - 1], s_ss.at[k], s_rs.at[k], dp=to * GROUP + mine_b
            )
        )
    for copy in sum_copies:
        copy.start()
    for copy in sum_copies:
        copy.wait_recv()
    grad = sum_send[mine_a].astype(F32)
    for k in range(1, n_class):
        grad = grad + sum_got[k - 1].astype(F32)

    first_new = beta_one * mom[0] + (1.0 - beta_one) * grad
    second_new = beta_two * mom[1] + (1.0 - beta_two) * grad * grad
    update = first_new / bias_one / (jnp.sqrt(second_new / bias_two) + adam_eps)
    my_place = mine_b * n_class + mine_a
    upd_all[my_place] = update.astype(BF16)

    upd_copies = []
    for k in range(1, n_class):
        to = lax.rem(mine_a + k, n_class)
        upd_copies.append(
            remote(
                upd_all.at[my_place],
                upd_all.at[my_place],
                u_ss.at[k],
                u_rs.at[k],
                dp=to * GROUP + mine_b,
            )
        )
    for copy in upd_copies:
        copy.start()

    mom[0] = first_new
    mom[1] = second_new
    for o in range(per_chunk):
        for l in range(wide):
            lanes = slice(o * ff + l * LANES, o * ff + (l + 1) * LANES)
            row = l * per_chunk + o
            first_ref[:, lanes] = mom[0, row : row + 1, :]
            second_ref[:, lanes] = mom[1, row : row + 1, :]

    for k in range(1, n_class):
        source = lax.rem(mine_a + n_class - k, n_class)
        spot = mine_b * n_class + source
        remote(
            upd_all.at[spot], upd_all.at[spot], u_ss.at[k], u_rs.at[k], dp=source * GROUP + mine_b
        ).wait_recv()
    class_copies = []
    for k in range(1, GROUP):
        to = lax.rem(mine_b + k, GROUP)
        span = pl.ds(mine_b * n_class, n_class)
        class_copies.append(
            remote(
                upd_all.at[span],
                upd_all.at[span],
                v_ss.at[k],
                v_rs.at[k],
                dp=mine_a * GROUP + to,
            )
        )
    for copy in class_copies:
        copy.start()

    def back_wait(k, carry):
        came = lax.rem(ep + k, n_ep)
        remote(
            back_send.at[k], back_got.at[came], b_ss.at[k], b_rs.at[k], ep=came
        ).wait_recv()
        return carry

    pltpu.make_async_copy(back_send.at[0], back_got.at[ep], b_rs.at[0]).wait()
    lax.fori_loop(1, n_ep, back_wait, 0)
    for at, size in blocks_of(width, 512):
        block = back_got[:, :, at : at + size].reshape(slots, size)
        rows_ref[:, at : at + size] = dot(gather, block).astype(BF16)

    for k in range(1, GROUP):
        source = lax.rem(mine_b + GROUP - k, GROUP)
        span = pl.ds(source * n_class, n_class)
        remote(
            upd_all.at[span], upd_all.at[span], v_ss.at[k], v_rs.at[k], dp=mine_a * GROUP + source
        ).wait_recv()
    chunk_wide[...] = upd_all[...].astype(F32).reshape(n_dp * chunk_rows, LANES)
    for j in range(n_dp):
        for l in range(wide):
            at = j * chunk_rows + l * per_chunk
            upd_pad[8 * j : 8 * j + 8, l * LANES : (l + 1) * LANES] = chunk_wide[at : at + 8, :]
    steps = dot(steps_lhs, upd_pad[...].astype(BF16)).astype(BF16)
    step_gate_ref[...] = steps[0:slab]
    step_up_ref[...] = steps[slab : 2 * slab]
    step_down_ref[...] = steps[2 * slab : 3 * slab]

    def sent_wait(k, carry):
        to = lax.rem(ep + k, n_ep)
        remote(x_send.at[to], x_got.at[k], x_ss.at[k], x_rs.at[k], ep=to).wait_send()
        remote(g_send.at[to], g_got.at[k], g_ss.at[k], g_rs.at[k], ep=to).wait_send()
        back_copy(k).wait_send()
        return carry

    lax.fori_loop(1, n_ep, sent_wait, 0)
    for copy in part_copies + sum_copies + upd_copies + class_copies:
        copy.wait_send()


def local(rows_in, grads_in, expert_ids, w_gate, w_up, w_down, project, moment_one, moment_two):
    n_ep = lax.axis_size("ep")
    n_dp = lax.axis_size("dp")
    rows_dev, width = rows_in.shape
    ff = w_gate.shape[2]
    rank = project.shape[3]
    slots = n_ep * CAP
    share = moment_one.shape[1]
    chunk_rows = -(-share // (LANES * 16)) * 16
    n_class = n_dp // GROUP
    slab = width // n_dp
    scale = 1.0 / math.sqrt(rows_dev * n_ep * n_dp)
    vmem = pl.BlockSpec(memory_space=pltpu.VMEM)
    anywhere = pl.BlockSpec(memory_space=pl.ANY)
    dma = pltpu.SemaphoreType.DMA
    outs = pl.pallas_call(
        functools.partial(kernel, n_ep, n_dp, scale),
        out_shape=(
            jax.ShapeDtypeStruct((rows_dev, width), BF16),
            jax.ShapeDtypeStruct((1, share), F32),
            jax.ShapeDtypeStruct((1, share), F32),
            jax.ShapeDtypeStruct((slab, ff), BF16),
            jax.ShapeDtypeStruct((slab, ff), BF16),
            jax.ShapeDtypeStruct((slab, ff), BF16),
        ),
        in_specs=[vmem] * 3 + [anywhere] * 6,
        out_specs=(vmem,) * 6,
        scratch_shapes=[
            pltpu.VMEM((rows_dev, width), BF16),
            pltpu.VMEM((rows_dev, width), BF16),
            pltpu.VMEM((width, ff), BF16),
            pltpu.VMEM((width, ff), BF16),
            pltpu.VMEM((ff, width), BF16),
            pltpu.VMEM((2, rank, width), BF16),
            *[pltpu.VMEM((n_ep, CAP, width), BF16)] * 6,
            pltpu.VMEM((slots, ff), F32),
            pltpu.VMEM((slots, ff), F32),
            pltpu.VMEM((slots, ff), BF16),
            pltpu.VMEM((slots, 2 * ff), BF16),
            pltpu.VMEM((8 * n_dp, ff), F32),
            pltpu.VMEM((n_dp * chunk_rows, LANES), F32),
            pltpu.VMEM((n_dp, chunk_rows, LANES), BF16),
            pltpu.VMEM((GROUP - 1, n_class, chunk_rows, LANES), BF16),
            pltpu.VMEM((n_class, chunk_rows, LANES), BF16),
            pltpu.VMEM((n_class - 1, chunk_rows, LANES), BF16),
            pltpu.VMEM((n_dp, chunk_rows, LANES), BF16),
            pltpu.VMEM((8 * n_dp, ff), F32),
            pltpu.VMEM((2, chunk_rows, LANES), F32),
            dma((6,)),
            *[dma((n_ep,))] * 6,
            *[dma((GROUP,))] * 2,
            *[dma((n_class,))] * 4,
            *[dma((GROUP,))] * 2,
        ],
        compiler_params=pltpu.CompilerParams(
            collective_id=0, has_side_effects=True, vmem_limit_bytes=48 << 20
        ),
        cost_estimate=pl.CostEstimate(
            flops=10 * slots * width * ff,
            bytes_accessed=6 * width * ff + 12 * rows_dev * width,
            transcendentals=slots * ff,
        ),
    )(
        expert_ids.reshape(1, rows_dev),
        moment_one,
        moment_two,
        rows_in,
        grads_in,
        w_gate[0],
        w_up[0],
        w_down[0],
        jnp.swapaxes(project[0], 1, 2),
    )
    rows_out, first_new, second_new, step_gate, step_up, step_down = outs
    return (
        rows_out,
        first_new,
        second_new,
        step_gate[None],
        step_up[None],
        jnp.swapaxes(step_down, 0, 1)[None],
    )


def solution(mesh):
    in_specs = (
        P(("ep", "dp"), None),
        P(("ep", "dp"), None),
        P(("ep", "dp"), None),
        P("ep", None, None),
        P("ep", None, None),
        P("ep", None, None),
        P("ep", None, None, None),
        P("ep", "dp"),
        P("ep", "dp"),
    )
    out_specs = (
        P(("ep", "dp"), None),
        P("ep", "dp"),
        P("ep", "dp"),
        P("ep", "dp", None),
        P("ep", "dp", None),
        P("ep", None, "dp"),
    )
    return jax.shard_map(local, mesh=mesh, in_specs=in_specs, out_specs=out_specs, check_vma=False)
```

time: 457 us -> 115 us (0.25)
  waiting for transfers between devices: 251 us -> 0 us
  blocking collectives: 115 us -> 0 us
  Pallas kernels: 0 us -> 102 us
  starting transfers between devices: 31.3 us -> 0 us
  matrix products: 23.5 us -> 0 us
  between operations: 14.2 us -> 0.66 us
  other arithmetic: 6.67 us -> 0 us
    psum x1 -> x0, waiting for transfers between devices: 244 us -> none  [local(): grad_sum = lax.psum(grad_flat, 'dp')]
    all_gather x2 -> x0, blocking collectives: 115 us -> none  [the longest x1 60.7 us: local(): lax.all_gather(moment_one, 'dp', axis=1, tiled=True)]
    pallas_call x0 -> x1, Pallas kernels: none -> 102 us  [local(): pl.pallas_call(functools.partial(kernel, n_ep, n_dp, scale), out_shape=(j...]
    all_to_all x3 -> x0, starting transfers between devices: 31.3 us -> none  [the longest x1 17.5 us: local(): lax.all_to_all(send_rows, 'ep', split_axis=0, concat_axis=0, tiled=True)]
    dot_general x13 -> x0, matrix products: 23.5 us -> none  [the longest x1 3.63 us: backward_pass(): jnp.einsum('sd,fd->sf', rows_g, down_mat, preferred_element_type=jnp.floa...]
    unnamed x18 -> x20, local copies, waits for them, and re-layouts: 0.05 us -> 10.8 us
    all_to_all x3 -> x0, waiting for transfers between devices: 7.3 us -> none  [the longest x1 7.29 us: local(): lax.all_to_all(send_grads, 'ep', split_axis=0, concat_axis=0, tiled=True)]
    scatter x2 -> x0, local copies, waits for them, and re-layouts: 5.91 us -> none  [the longest x1 2.96 us: local(): send_grads = empty_slots.at[places].set(grads_in)]
  transfers between devices with their start and end apart: 4 -> 0, of which waited for: 2 -> 0; matrix products, arithmetic and copies ran while one was open for 6% -> 0% of each run, Pallas kernels for 0% -> 0%
where the time goes in v1:
time: 115 us; the launch traced here: 114 us
  Pallas kernels  102 us (89%)
  local copies, waits for them, and re-layouts  10.8 us (9%)
    pallas_call x1, Pallas kernels, local(): pl.pallas_call(functools.partial(kernel, n_ep, n_dp, scale), out_shape=(j...  102 us
    unnamed x20, local copies, waits for them, and re-layouts  10.8 us

profile of v1, /device:TPU:6, one launch (start us, length us, event | category | flops | bytes accessed | tf_op | source)
XLA Modules:
  0.0 113.7 jit_solution(8219420531219776696)
XLA Ops:
  0.6 0.0 copy-start
  0.6 1.7 %copy-done = bf16[1,2048,640]{2,1,0:T(8,128)(2,1)S(1)} copy-done((bf16[1,2048,640]{2,1,0:T(8,128)(2,1)S(1)}, bf16[1,2048,640]{2,1,0:T(8,128)(2,1)}, u32[]{:S(2)}) %copy-start) | copy-done | bytes 2621464
  2.4 0.0 copy-start.1
  2.4 1.0 copy-done.1
  3.4 0.0 copy-start.2
  3.4 1.0 copy-done.2
  4.5 0.0 copy-start.3
  4.5 1.0 copy-done.3
  5.5 0.0 copy-start.4
  5.5 0.7 copy-done.4
  6.2 0.0 copy-start.5
  6.2 0.7 copy-done.5
  6.9 0.0 copy-start.6
  6.9 0.7 copy-done.6
  7.6 102.2 %shard_map.136 = (bf16[128,2048]{1,0:T(8,128)(2,1)S(1)}, f32[1,3840]{1,0:T(1,128)S(1)}, f32[1,3840]{1,0:T(1,128)S(1)}, bf16[64,640]{1,0:T(8,128)(2,1)S(1)}, bf16...) custom-call(s32[1,128]{1,0:T(1,128)S(1)} %bitcast.17, f32[1,3840]{1,0:T(1,128)S(1)} %copy-done.4, ...), custom_call_target="tpu_custom_call" | custom-call | flops 3355443200 | bytes 11010048 | tf_op jit(solution)/shard_map/pallas_call | solution.py:442
  109.8 0.8 copy.21
  110.6 0.6 copy.22
  111.2 0.6 copy.23
  111.8 0.6 copy.24
  112.4 0.6 copy.25
  113.1 0.6 copy.26
Async XLA Ops:
  0.6 1.7 %copy-start = (bf16[1,2048,640]{2,1,0:T(8,128)(2,1)S(1)}, bf16[1,2048,640]{2,1,0:T(8,128)(2,1)}, u32[]{:S(2)}) copy-start(bf16[1,2048,640]{2,1,0:T(8,128)(2,1)} %param.12) | copy-start | bytes 7864324
  2.4 1.0 copy-start.1
  3.4 1.0 copy-start.2
  4.5 1.0 copy-start.3
  5.5 0.7 copy-start.4
  6.2 0.7 copy-start.5
  6.9 0.7 copy-start.6

commit v2 on v1

--- a/solution.py
+++ b/solution.py
@@ -53,9 +53,9 @@
     n_ep,
     n_dp,
     scale,
-    ids_ref,
-    m1_ref,
-    m2_ref,
+    ids_hbm,
+    m1_hbm,
+    m2_hbm,
     x_hbm,
     g_hbm,
     wg_hbm,
@@ -65,9 +65,11 @@
     rows_ref,
     first_ref,
     second_ref,
-    step_gate_ref,
-    step_up_ref,
-    step_down_ref,
+    upd_all,
+    lhs_ref,
+    ids_ref,
+    m1_ref,
+    m2_ref,
     x_in,
     g_in,
     wg,
@@ -90,8 +92,6 @@
     part_got,
     sum_send,
     sum_got,
-    upd_all,
-    upd_pad,
     mom,
     local_sem,
     x_ss,
@@ -108,6 +108,7 @@
     u_rs,
     v_ss,
     v_rs,
+    near,
 ):
     ep = lax.axis_index("ep")
     dp = lax.axis_index("dp")
@@ -131,7 +132,12 @@
         pltpu.make_async_copy(wu_hbm, wu, local_sem.at[4]),
         pltpu.make_async_copy(wd_hbm, wd, local_sem.at[5]),
     ]
-    for load in loads:
+    small = [
+        pltpu.make_async_copy(ids_hbm, ids_ref, local_sem.at[6]),
+        pltpu.make_async_copy(m1_hbm, m1_ref, local_sem.at[7]),
+        pltpu.make_async_copy(m2_hbm, m2_ref, local_sem.at[8]),
+    ]
+    for load in small[0:1] + loads + small[1:]:
         load.start()
 
     barrier = pltpu.get_barrier_semaphore()
@@ -143,13 +149,18 @@
         return carry
 
     lax.fori_loop(1, n_ep, greet, 0)
-    for k in range(1, GROUP):
-        peer = mine_a * GROUP + lax.rem(mine_b + k, GROUP)
-        pl.semaphore_signal(barrier, inc=1, device_id={"dp": peer}, device_id_type=MESH)
-    for k in range(1, n_class):
-        peer = lax.rem(mine_a + k, n_class) * GROUP + mine_b
-        pl.semaphore_signal(barrier, inc=1, device_id={"dp": peer}, device_id_type=MESH)
-
+    def tell(semaphore, offset):
+        pl.semaphore_signal(
+            semaphore,
+            inc=1,
+            device_id={"dp": lax.rem(dp + offset, n_dp)},
+            device_id_type=MESH,
+        )
+
+    tell(barrier, 1)
+    tell(barrier, n_dp - 1)
+
+    small[0].wait()
     ids = ids_ref[...]
     named = (lax.broadcasted_iota(jnp.int32, (n_ep, rows_dev), 0) == ids).astype(F32)
     before = lax.broadcasted_iota(jnp.int32, (rows_dev, rows_dev), 0) < lax.broadcasted_iota(
@@ -193,7 +204,10 @@
 
     loads[0].wait()
     scatter(x_in, x_send)
-    pl.semaphore_wait(barrier, (n_ep - 1) + (GROUP - 1) + (n_class - 1))
+    pl.semaphore_wait(barrier, (n_ep - 1) + 2)
+    rounds = [1 << r for r in range((n_dp // 4).bit_length())]
+    tell(near.at[0, 0], rounds[0])
+    tell(near.at[0, 1], n_dp - rounds[0])
     send_all(x_send, x_got, x_ss, x_rs)
     loads[1].wait()
     scatter(g_in, g_send)
@@ -223,7 +237,9 @@
         for other in range(1, LANES // slab):
             chosen = jnp.where(part_at == other, both[other * slab : (other + 1) * slab], chosen)
         steps_lhs.append(chosen.astype(BF16))
-    steps_lhs = jnp.concatenate(steps_lhs, axis=0)
+    lhs_ref[...] = jnp.concatenate(steps_lhs, axis=0)
+    small[1].wait()
+    small[2].wait()
     mom[...] = jnp.zeros_like(mom)
     for o in range(per_chunk):
         for l in range(wide):
@@ -232,6 +248,12 @@
             mom[0, row : row + 1, :] = m1_ref[:, lanes]
             mom[1, row : row + 1, :] = m2_ref[:, lanes]
 
+    for r in range(len(rounds)):
+        pl.semaphore_wait(near.at[r, 0], 1)
+        pl.semaphore_wait(near.at[r, 1], 1)
+        if r + 1 < len(rounds):
+            tell(near.at[r + 1, 0], rounds[r + 1])
+            tell(near.at[r + 1, 1], n_dp - rounds[r + 1])
     loads[3].wait()
     loads[4].wait()
     loads[5].wait()
@@ -307,7 +329,6 @@
         back_copy(k).start()
         return carry
 
-    lax.fori_loop(1, n_ep, back_start, 0)
 
     for copy in part_copies:
         copy.wait_recv()
@@ -325,6 +346,7 @@
         )
     for copy in sum_copies:
         copy.start()
+    lax.fori_loop(1, n_ep, back_start, 0)
     for copy in sum_copies:
         copy.wait_recv()
     grad = sum_send[mine_a].astype(F32)
@@ -402,16 +424,6 @@
         remote(
             upd_all.at[span], upd_all.at[span], v_ss.at[k], v_rs.at[k], dp=mine_a * GROUP + source
         ).wait_recv()
-    chunk_wide[...] = upd_all[...].astype(F32).reshape(n_dp * chunk_rows, LANES)
-    for j in range(n_dp):
-        for l in range(wide):
-            at = j * chunk_rows + l * per_chunk
-            upd_pad[8 * j : 8 * j + 8, l * LANES : (l + 1) * LANES] = chunk_wide[at : at + 8, :]
-    steps = dot(steps_lhs, upd_pad[...].astype(BF16)).astype(BF16)
-    step_gate_ref[...] = steps[0:slab]
-    step_up_ref[...] = steps[slab : 2 * slab]
-    step_down_ref[...] = steps[2 * slab : 3 * slab]
-
     def sent_wait(k, carry):
         to = lax.rem(ep + k, n_ep)
         remote(x_send.at[to], x_got.at[k], x_ss.at[k], x_rs.at[k], ep=to).wait_send()
@@ -422,6 +434,52 @@
     lax.fori_loop(1, n_ep, sent_wait, 0)
     for copy in part_copies + sum_copies + upd_copies + class_copies:
         copy.wait_send()
+
+
+def finish(n_dp, per_chunk, rows_in, first_in, second_in, upd_in, lhs_in, *refs):
+    rows_out, first_out, second_out, step_gate, step_up, step_down = refs[0:6]
+    upd_all, lhs, rows, first, second, wide_upd, upd_pad, steps, in_sem, out_sem = refs[6:]
+    fetch = [
+        pltpu.make_async_copy(source, target, in_sem.at[n])
+        for n, (source, target) in enumerate(
+            (
+                (upd_in, upd_all),
+                (lhs_in, lhs),
+                (rows_in, rows),
+                (first_in, first),
+                (second_in, second),
+            )
+        )
+    ]
+    for copy in fetch:
+        copy.start()
+    early = [
+        pltpu.make_async_copy(rows, rows_out, out_sem.at[0]),
+        pltpu.make_async_copy(first, first_out, out_sem.at[1]),
+        pltpu.make_async_copy(second, second_out, out_sem.at[2]),
+    ]
+    fetch[0].wait()
+    fetch[1].wait()
+    chunk_rows = upd_all.shape[1]
+    ff = upd_pad.shape[1]
+    slab = step_gate.shape[0]
+    wide_upd[...] = upd_all[...].astype(F32).reshape(n_dp * chunk_rows, LANES)
+    for j in range(n_dp):
+        for l in range(ff // LANES):
+            at = j * chunk_rows + l * per_chunk
+            upd_pad[8 * j : 8 * j + 8, l * LANES : (l + 1) * LANES] = wide_upd[at : at + 8, :]
+    for copy in fetch[2:]:
+        copy.wait()
+    for copy in early:
+        copy.start()
+    late = []
+    steps[...] = dot(lhs[...], upd_pad[...].astype(BF16)).reshape(3, slab, ff).astype(BF16)
+    for kind, out in enumerate((step_gate, step_up, step_down)):
+        late.append(pltpu.make_async_copy(steps.at[kind], out, out_sem.at[3 + kind]))
+    for copy in late:
+        copy.start()
+    for copy in early + late:
+        copy.wait()
 
 
 def local(rows_in, grads_in, expert_ids, w_gate, w_up, w_down, project, moment_one, moment_two):
@@ -437,7 +495,7 @@
     slab = width // n_dp
     scale = 1.0 / math.sqrt(rows_dev * n_ep * n_dp)
     vmem = pl.BlockSpec(memory_space=pltpu.VMEM)
-    anywhere = pl.BlockSpec(memory_space=pl.ANY)
+    hbm = pl.BlockSpec(memory_space=pltpu.HBM)
     dma = pltpu.SemaphoreType.DMA
     outs = pl.pallas_call(
         functools.partial(kernel, n_ep, n_dp, scale),
@@ -445,13 +503,15 @@
             jax.ShapeDtypeStruct((rows_dev, width), BF16),
             jax.ShapeDtypeStruct((1, share), F32),
             jax.ShapeDtypeStruct((1, share), F32),
-            jax.ShapeDtypeStruct((slab, ff), BF16),
-            jax.ShapeDtypeStruct((slab, ff), BF16),
-            jax.ShapeDtypeStruct((slab, ff), BF16),
+            jax.ShapeDtypeStruct((n_dp, chunk_rows, LANES), BF16),
+            jax.ShapeDtypeStruct((3 * slab, 8 * n_dp), BF16),
         ),
-        in_specs=[vmem] * 3 + [anywhere] * 6,
-        out_specs=(vmem,) * 6,
+        in_specs=[hbm] * 9,
+        out_specs=(vmem,) * 5,
         scratch_shapes=[
+            pltpu.VMEM((1, rows_dev), jnp.int32),
+            pltpu.VMEM((1, share), F32),
+            pltpu.VMEM((1, share), F32),
             pltpu.VMEM((rows_dev, width), BF16),
             pltpu.VMEM((rows_dev, width), BF16),
             pltpu.VMEM((width, ff), BF16),
@@ -469,17 +529,16 @@
             pltpu.VMEM((GROUP - 1, n_class, chunk_rows, LANES), BF16),
             pltpu.VMEM((n_class, chunk_rows, LANES), BF16),
             pltpu.VMEM((n_class - 1, chunk_rows, LANES), BF16),
-            pltpu.VMEM((n_dp, chunk_rows, LANES), BF16),
-            pltpu.VMEM((8 * n_dp, ff), F32),
             pltpu.VMEM((2, chunk_rows, LANES), F32),
-            dma((6,)),
+            dma((9,)),
             *[dma((n_ep,))] * 6,
             *[dma((GROUP,))] * 2,
             *[dma((n_class,))] * 4,
             *[dma((GROUP,))] * 2,
+            pltpu.SemaphoreType.REGULAR((max(1, n_dp.bit_length() - 2), 2)),
         ],
         compiler_params=pltpu.CompilerParams(
-            collective_id=0, has_side_effects=True, vmem_limit_bytes=48 << 20
+            collective_id=0, has_side_effects=True, vmem_limit_bytes=60 << 20
         ),
         cost_estimate=pl.CostEstimate(
             flops=10 * slots * width * ff,
@@ -497,7 +556,32 @@
         w_down[0],
         jnp.swapaxes(project[0], 1, 2),
     )
-    rows_out, first_new, second_new, step_gate, step_up, step_down = outs
+    rows_out, first_new, second_new, step_gate, step_up, step_down = pl.pallas_call(
+        functools.partial(finish, n_dp, 3 * rank // n_dp),
+        out_shape=(
+            jax.ShapeDtypeStruct((rows_dev, width), BF16),
+            jax.ShapeDtypeStruct((1, share), F32),
+            jax.ShapeDtypeStruct((1, share), F32),
+            jax.ShapeDtypeStruct((slab, ff), BF16),
+            jax.ShapeDtypeStruct((slab, ff), BF16),
+            jax.ShapeDtypeStruct((slab, ff), BF16),
+        ),
+        in_specs=[hbm] * 5,
+        out_specs=(hbm,) * 6,
+        scratch_shapes=[
+            pltpu.VMEM((n_dp, chunk_rows, LANES), BF16),
+            pltpu.VMEM((3 * slab, 8 * n_dp), BF16),
+            pltpu.VMEM((rows_dev, width), BF16),
+            pltpu.VMEM((1, share), F32),
+            pltpu.VMEM((1, share), F32),
+            pltpu.VMEM((n_dp * chunk_rows, LANES), F32),
+            pltpu.VMEM((8 * n_dp, ff), F32),
+            pltpu.VMEM((3, slab, ff), BF16),
+            dma((5,)),
+            dma((6,)),
+        ],
+        compiler_params=pltpu.CompilerParams(vmem_limit_bytes=60 << 20),
+    )(*outs)
     return (
         rows_out,
         first_new,

time: 115 us -> 96.9 us (0.84)
  the two profiles are of different devices: /device:TPU:6 before, /device:TPU:4 now
where the time goes in v2:
time: 96.9 us; the launch traced here: 96.7 us
  Pallas kernels  96.1 us (99%)
    pallas_call x1, Pallas kernels, local(): pl.pallas_call(functools.partial(kernel, n_ep, n_dp, scale), out_shape=(j...  93.9 us
    pallas_call x1, Pallas kernels, local(): pl.pallas_call(functools.partial(finish, n_dp, 3 * rank // n_dp), out_sha...  2.2 us

profile of v2, /device:TPU:4, one launch (start us, length us, event | category | flops | bytes accessed | tf_op | source)
XLA Modules:
  0.0 96.7 jit_solution(15667903057141710081)
XLA Ops:
  0.6 93.9 %shard_map.136 = (bf16[128,2048]{1,0:T(8,128)(2,1)}, f32[1,3840]{1,0:T(1,128)}, f32[1,3840]{1,0:T(1,128)}, bf16[32,32,128]{2,1,0:T(8,128)(2,1)}, bf16[192,256]{1,0:T(8,128)(2,1)}) custom-call(s32[1,128]{1,0:T(1,128)} %bitcast.19, f32[1,3840]{1,0:T(1,128)} %m1_hbm.1, f32[1,3840]{1,0:T(1,128)} %m2_hbm.1, bf16[128,2048]{1,0:T(8,128)(2,1)} %x_hbm.1, ...), custom_call_target="tpu_custom_call" | custom-call | flops 3355443200 | bytes 11010048 | tf_op jit(solution)/shard_map/pallas_call | solution.py:500
  94.5 2.2 %shard_map.137 = (bf16[128,2048]{1,0:T(8,128)(2,1)}, f32[1,3840]{1,0:T(1,128)}, f32[1,3840]{1,0:T(1,128)}, bf16[64,640]{1,0:T(8,128)(2,1)}, bf16[64,640]{1,0:T(8,128)(2,1)}, /*index=5*/bf16[64,640]{1,0:T(8,128)(2,1)}) custom-call(bf16[128,2048]{1,0:T(8,128)(2,1)} %get-tuple-element.17.rows_in, f32[1,3840]{1,0:T(1,128)} %get-tuple-element.18.first_in, ...), custom_call_target="tpu_custom_call" | custom-call | tf_op jit(solution)/shard_map/pallas_call | solution.py:559

commit v3 on v2

--- a/solution.py
+++ b/solution.py
@@ -18,6 +18,7 @@
 CAP = 8
 GROUP = 4
 LANES = 128
+STRIDE = 13
 F32 = jnp.float32
 BF16 = jnp.bfloat16
 
@@ -181,7 +182,8 @@
     def send_all(source, target, send_sems, recv_sems):
         pltpu.make_async_copy(source.at[ep], target.at[0], recv_sems.at[0]).start()
 
-        def one(k, carry):
+        def one(turn, carry):
+            k = lax.rem(turn * STRIDE, n_ep)
             to = lax.rem(ep + k, n_ep)
             remote(
                 source.at[to], target.at[k], send_sems.at[k], recv_sems.at[k], ep=to
@@ -325,8 +327,8 @@
         to = lax.rem(ep + n_ep - k, n_ep)
         return remote(back_send.at[k], back_got.at[ep], b_ss.at[k], b_rs.at[k], ep=to)
 
-    def back_start(k, carry):
-        back_copy(k).start()
+    def back_start(turn, carry):
+        back_copy(lax.rem(turn * STRIDE, n_ep)).start()
         return carry
 
 

time: 96.9 us -> 92.6 us (0.956)
  the two profiles are of different devices: /device:TPU:4 before, /device:TPU:6 now
where the time goes in v3:
time: 92.6 us; the launch traced here: 92.4 us
  Pallas kernels  91.8 us (99%)
    pallas_call x1, Pallas kernels, local(): pl.pallas_call(functools.partial(kernel, n_ep, n_dp, scale), out_shape=(j...  89.6 us
    pallas_call x1, Pallas kernels, local(): pl.pallas_call(functools.partial(finish, n_dp, 3 * rank // n_dp), out_sha...  2.2 us

profile of v3, /device:TPU:6, one launch (start us, length us, event | category | flops | bytes accessed | tf_op | source)
XLA Modules:
  0.0 92.4 jit_solution(16783825349435663734)
XLA Ops:
  0.6 89.6 %shard_map.136 = (bf16[128,2048]{1,0:T(8,128)(2,1)}, f32[1,3840]{1,0:T(1,128)}, f32[1,3840]{1,0:T(1,128)}, bf16[32,32,128]{2,1,0:T(8,128)(2,1)}, bf16[192,256]{1,0:T(8,128)(2,1)}) custom-call(s32[1,128]{1,0:T(1,128)} %bitcast.19, f32[1,3840]{1,0:T(1,128)} %m1_hbm.1, f32[1,3840]{1,0:T(1,128)} %m2_hbm.1, bf16[128,2048]{1,0:T(8,128)(2,1)} %x_hbm.1, ...), custom_call_target="tpu_custom_call" | custom-call | flops 3355443200 | bytes 11010048 | tf_op jit(solution)/shard_map/pallas_call | solution.py:502
  90.2 2.2 %shard_map.137 = (bf16[128,2048]{1,0:T(8,128)(2,1)}, f32[1,3840]{1,0:T(1,128)}, f32[1,3840]{1,0:T(1,128)}, bf16[64,640]{1,0:T(8,128)(2,1)}, bf16[64,640]{1,0:T(8,128)(2,1)}, /*index=5*/bf16[64,640]{1,0:T(8,128)(2,1)}) custom-call(bf16[128,2048]{1,0:T(8,128)(2,1)} %get-tuple-element.17.rows_in, f32[1,3840]{1,0:T(1,128)} %get-tuple-element.18.first_in, ...), custom_call_target="tpu_custom_call" | custom-call | tf_op jit(solution)/shard_map/pallas_call | solution.py:561
